TPU v7x, 32 devices: a whole 2x2x4 slice. The times are simulated.
32 devices in a mesh: row: 8 (over y, x, core), col: 4 (over z).
Axes of the slice: x: 2, y: 2, z: 4, core: 2. Of those that a mesh axis runs over, the one named last changes fastest.
Arguments:
- features: bfloat16 [32, 1024, 1024], P(None, 'row', 'col'), may hold values from -45 to 45
- first_kernel: bfloat16 [3, 3, 32, 32], replicated, may hold values from -0.375 to 0.375
- second_kernel: bfloat16 [3, 3, 32, 32], replicated, may hold values from -0.375 to 0.375
- first_gain: float32 [32], replicated, may hold values from 0.5 to 1.5
- first_shift: float32 [32], replicated, may hold values from -3 to 3
- second_gain: float32 [32], replicated, may hold values from 0.5 to 1.5
- second_shift: float32 [32], replicated, may hold values from -3 to 3
Outputs:
- symmetric_map: bfloat16 [32, 1024, 1024], P(None, 'row', 'col')
All inputs are finite; a program needn't handle non-finite values.
Results may differ from a plain program's by a relative error of at most 0.0053.
Values may be sent and summed in bfloat16 or wider, within the bound.
A program may use at most 192 MiB of HBM per device.

v0:
```python
import jax
import jax.numpy as jnp
from jax import lax
from jax.sharding import PartitionSpec as P

DILATION_STEP = 8
epsilon = 1e-05


def with_halo(cells, sides, width):
    for axis, dim in sides:
        count = lax.axis_size(axis)
        ends = count - 1
        head = lax.slice_in_dim(cells, 0, width, axis=dim)
        tail = lax.slice_in_dim(cells, cells.shape[dim] - width, cells.shape[dim], axis=dim)
        cells = jnp.concatenate(
            [
                lax.ppermute(tail, axis, [(i, (i + 1) % count) for i in range(ends)]),
                cells,
                lax.ppermute(head, axis, [((i + 1) % count, i) for i in range(ends)]),
            ],
            axis=dim,
        )
    return cells


def apply_taps(padded, kernels, output_rows, output_columns):
    members = padded.shape[0]
    channels = kernels.shape[3]
    total = jnp.zeros((members, channels, output_rows, output_columns), jnp.float32)
    for filter_row in range(3):
        for filter_column in range(3):
            piece = padded[
                :,
                :,
                filter_row * DILATION_STEP : filter_row * DILATION_STEP + output_rows,
                filter_column * DILATION_STEP : filter_column * DILATION_STEP + output_columns,
            ]
            total = total + jnp.einsum(
                "poc,pchw->pohw",
                kernels[:, filter_row, filter_column],
                piece,
                preferred_element_type=jnp.float32,
            )
    return total


def extend(receptive_field):
    return with_halo(receptive_field, (("row", 2), ("col", 3)), DILATION_STEP)


def channel_affine(inner, gain, total_cells):
    sums = lax.psum(jnp.sum(inner, axis=(1, 2)), ("row", "col"))
    centre = sums / total_cells
    deviation = inner - centre[:, None, None]
    spread = lax.psum(jnp.sum(deviation * deviation, axis=(1, 2)), ("row", "col")) / total_cells
    factor = gain * lax.rsqrt(spread + epsilon)
    return (centre, factor)


def apply_norm(hidden, centre, factor, shift):
    return (hidden - centre[:, None, None]) * factor[:, None, None] + shift[:, None, None]


def residual_block(
    stacked, first_stack, second_stack, first_gain, first_shift, second_gain, second_shift
):
    tile_rows = stacked.shape[2]
    tile_cols = stacked.shape[3]
    row_devs = lax.axis_size("row")
    col_devs = lax.axis_size("col")
    total_cells = float(tile_rows * tile_cols * row_devs * col_devs)
    first = apply_taps(extend(stacked), first_stack, tile_rows, tile_cols)
    centre, factor = channel_affine(first[0], first_gain, total_cells)
    active = jnp.maximum(apply_norm(first, centre, factor, first_shift), 0.0).astype(jnp.bfloat16)
    second = apply_taps(extend(active), second_stack, tile_rows, tile_cols)
    centre_two, factor_two = channel_affine(second[0], second_gain, total_cells)
    return (
        stacked.astype(jnp.float32) + apply_norm(second, centre_two, factor_two, second_shift)
    ).astype(jnp.bfloat16)


def mirror(block):
    row_devs = lax.axis_size("row")
    col_devs = lax.axis_size("col")
    channels, tile_rows, tile_cols = block.shape
    ratio = row_devs // col_devs
    slab_rows = tile_rows // col_devs
    banded = lax.all_to_all(block, "col", split_axis=1, concat_axis=2, tiled=True)
    moved = lax.all_to_all(
        lax.all_to_all(banded, "row", split_axis=2, concat_axis=1, tiled=True),
        "col",
        split_axis=1,
        concat_axis=1,
        tiled=True,
    )
    arranged = moved.reshape(channels, col_devs, ratio, slab_rows, tile_rows)
    arranged = jnp.transpose(arranged, (0, 2, 1, 3, 4)).reshape(channels, tile_cols, tile_rows)
    return jnp.swapaxes(arranged, 1, 2)


def per_device(
    features, first_kernel, second_kernel, first_gain, first_shift, second_gain, second_shift
):
    summed = residual_block(
        features[None],
        first_kernel[None],
        second_kernel[None],
        first_gain,
        first_shift,
        second_gain,
        second_shift,
    )[0]
    total = summed.astype(jnp.float32) + mirror(summed).astype(jnp.float32)
    return (total * 0.5).astype(jnp.bfloat16)


def solution(mesh):
    placed = (P(None, "row", "col"), P(), P(), P(), P(), P(), P())
    return jax.shard_map(
        per_device, mesh=mesh, in_specs=placed, out_specs=P(None, "row", "col"), check_vma=False
    )
```

profile of v0, /device:TPU:0, one launch (start us, length us, event | category | flops | bytes accessed | tf_op | source)
XLA Modules:
  0.0 518.0 jit_solution(3476700549415977012)
XLA Ops:
  0.0 2.9 copy.68
  6.6 4.0 fusion.30
  12.6 3.2 copy.40
  15.8 5.0 collective-permute-start.2
  24.4 3.4 fusion.18
  27.7 3.4 fusion.26
  31.1 2.6 copy.41
  33.7 3.4 copy.43
  37.1 7.1 %pad_maximum_fusion = (bf16[1,32,144,264]{3,1,2,0:T(8,128)(2,1)S(1)}, bf16[1,32,144,264]{3,1,2,0:T(8,128)(2,1)S(1)}) fusion(bf16[1,32,144,8]{3,1,2,0:T(8,128)(2,1)} %copy.43, bf16[1,32,8,256]{3,1,2,0:T(8,128)(2,1)S(1)} %collective-permute-done.1, bf16[1,32,128,256]{3,1,2,0:T(8,128)(2,1)S(1)} %bitcast.206, ...), kind=kLoop, calls=%fused_computation.16 | loop fusion | flops 19464192 | bytes 7372800 | tf_op jit(solution)/shard_map/concatenate | solution.py:16
  44.2 2.6 fusion.21
  46.8 2.6 fusion.23
  49.5 2.8 fusion.22
  52.2 2.8 fusion.24
  55.0 2.8 fusion.29
  58.6 12.7 %fusion.41 = (f32[32]{0:T(128)S(1)}, f32[32,128,256]{2,0,1:T(8,128)}) fusion(bf16[1,32,144,264]{3,1,2,0:T(8,128)(2,1)S(1)} %get-tuple-element.9, bf16[1,3,3,32,32]{4,3,2,1,0:T(8,128)(2,1)} %bitcast.217, f32[128,256,32]{1,2,0:T(8,128)S(1)} %copy-done.5, f32[128,256,32]{1,2,0:T(8,128)} %fusion.21, f32[128,256,32]{1,2,0:T(8,128)} %fusion.22, ...), kind=kOutput, calls=%fused_computation.95 | convolution fusion | flops 76546016 | bytes 39854208 | tf_op jit(solution)/shard_map/poc,pchw->pohw/dot_general | solution.py:39
  71.3 43.9 %psum.28 = f32[32]{0:T(128)S(1)} all-reduce(f32[32]{0:T(128)S(1)} %get-tuple-element.17), channel_id=1, replica_groups=mesh['row'=8,'col'=4] {'row','col'}, use_global_device_ids=true, to_apply=%region_1.0 | all-reduce | flops 32 | bytes 256 | tf_op jit(solution)/shard_map/psum | solution.py:53
  115.2 2.8 multiply_reduce_fusion.1
  118.0 53.8 %psum.29 = f32[32]{0:T(128)S(1)} all-reduce(f32[32]{0:T(128)S(1)} %multiply_reduce_fusion.1), channel_id=1, replica_groups=mesh['row'=8,'col'=4] {'row','col'}, use_global_device_ids=true, to_apply=%region_3.0 | all-reduce | flops 32 | bytes 256 | tf_op jit(solution)/shard_map/psum | solution.py:56
  171.8 3.1 fusion.44
  177.6 3.5 fusion.32
  183.9 3.2 copy.45
  187.2 2.7 collective-permute-start.6
  193.2 3.4 fusion.13
  196.6 3.3 fusion.5
  199.9 2.6 copy.46
  202.5 3.4 copy.48
  205.9 7.1 %pad_maximum_fusion.1 = (bf16[1,32,144,264]{3,1,2,0:T(8,128)(2,1)S(1)}, bf16[1,32,144,264]{3,1,2,0:T(8,128)(2,1)S(1)}) fusion(bf16[1,32,144,8]{3,1,2,0:T(8,128)(2,1)} %copy.48, bf16[1,32,8,256]{3,1,2,0:T(8,128)(2,1)S(1)} %collective-permute-done.5, bf16[1,32,128,256]{3,1,2,0:T(8,128)(2,1)S(1)} %fusion.44, ...), kind=kLoop, calls=%fused_computation.18 | loop fusion | flops 19464192 | bytes 7372800 | tf_op jit(solution)/shard_map/concatenate | solution.py:16
  213.1 2.6 fusion.10
  215.7 2.6 fusion.16
  218.3 2.6 fusion.8
  221.0 2.8 fusion.11
  223.7 2.8 fusion.9
  226.9 11.5 %fusion.42 = (f32[32]{0:T(128)S(1)}, f32[128,256,32]{1,2,0:T(8,128)}) fusion(bf16[1,32,144,264]{3,1,2,0:T(8,128)(2,1)S(1)} %get-tuple-element.5, bf16[1,3,3,32,32]{4,3,2,1,0:T(8,128)(2,1)} %bitcast.226, f32[128,256,32]{1,2,0:T(8,128)S(1)} %copy-done.7, f32[128,256,32]{1,2,0:T(8,128)} %fusion.8, f32[128,256,32]{1,2,0:T(8,128)} %fusion.9, ...), kind=kOutput, calls=%fused_computation.96 | convolution fusion | flops 76546016 | bytes 39854208 | tf_op jit(solution)/shard_map/poc,pchw->pohw/dot_general | solution.py:39
  238.5 43.7 %psum.30 = f32[32]{0:T(128)S(1)} all-reduce(f32[32]{0:T(128)S(1)} %get-tuple-element.19), channel_id=1, replica_groups=mesh['row'=8,'col'=4] {'row','col'}, use_global_device_ids=true, to_apply=%region_5.0 | all-reduce | flops 32 | bytes 256 | tf_op jit(solution)/shard_map/psum | solution.py:53
  282.2 2.8 multiply_reduce_fusion
  285.1 41.8 %psum.31 = f32[32]{0:T(128)S(1)} all-reduce(f32[32]{0:T(128)S(1)} %multiply_reduce_fusion), channel_id=1, replica_groups=mesh['row'=8,'col'=4] {'row','col'}, use_global_device_ids=true, to_apply=%region_7.0 | all-reduce | flops 32 | bytes 256 | tf_op jit(solution)/shard_map/psum | solution.py:56
  326.9 4.0 fusion.2
  330.9 50.7 %all_to_all.41 = bf16[32,128,256]{2,0,1:T(8,128)(2,1)S(1)} all-to-all(bf16[32,128,256]{2,0,1:T(8,128)(2,1)S(1)} %fusion.2), channel_id=1, replica_groups=mesh['row'=8,'col'=4] {'col'}, dimensions={1} | all-to-all | bytes 4194304 | tf_op jit(solution)/shard_map/all_to_all | solution.py:89
  383.3 7.1 %copy.58 = bf16[32,32,4,256]{1,0,3,2:T(8,128)(2,1)} copy(bf16[32,32,4,256]{3,2,1,0:T(4,128)(2,1)S(1)} %bitcast.210) | data formatting | bytes 4194304 | tf_op jit(solution)/shard_map/all_to_all | solution.py:89
  390.4 10.1 %reshape.252 = bf16[8,2,65536]{2,1,0:T(2,128)(2,1)S(1)} reshape(bf16[1024,32,32]{2,1,0:T(8,128)(2,1)} %bitcast.207) | data formatting | bytes 4194304
  400.5 30.1 %all_to_all.42 = bf16[8,2,65536]{2,1,0:T(2,128)(2,1)} all-to-all(bf16[8,2,65536]{2,1,0:T(2,128)(2,1)S(1)} %reshape.252), channel_id=1, replica_groups=mesh['row'=8,'col'=4] {'row'}, dimensions={0} | all-to-all | bytes 4194304 | tf_op jit(solution)/shard_map/all_to_all | solution.py:91
  430.6 8.7 %reshape.253 = bf16[1024,32,32]{2,1,0:T(8,128)(2,1)} reshape(bf16[8,2,65536]{2,1,0:T(2,128)(2,1)} %all_to_all.42) | data formatting | bytes 4194304
  439.3 12.6 %copy.61 = bf16[32,8,32,128]{3,0,2,1:T(8,128)(2,1)S(1)} copy(bf16[32,8,32,128]{2,0,3,1:T(8,128)(2,1)} %bitcast.208) | data formatting | bytes 4194304 | tf_op jit(solution)/shard_map/all_to_all | solution.py:91
  451.9 50.5 %all_to_all.43 = bf16[32,256,128]{2,0,1:T(8,128)(2,1)S(1)} all-to-all(bf16[32,256,128]{2,0,1:T(8,128)(2,1)S(1)} %bitcast.211), channel_id=1, replica_groups=mesh['row'=8,'col'=4] {'col'}, dimensions={1} | all-to-all | bytes 4194304 | tf_op jit(solution)/shard_map/all_to_all | solution.py:90
  503.8 2.6 copy.55
  506.4 5.6 %copy.56 = f32[32,256,128]{1,0,2:T(8,128)} copy(f32[32,256,128]{2,1,0:T(8,128)} %bitcast.209) | data formatting | bytes 8388608 | tf_op jit(solution)/shard_map/convert_element_type | solution.py:114
  512.0 3.0 fusion.1
  515.1 2.5 copy.57
  (57 shorter events, 22.3 us)
Async XLA Ops:
  0.0 6.6 %copy-start.1 = (bf16[32,128,256]{2,1,0:T(8,128)(2,1)S(1)}, bf16[32,128,256]{2,1,0:T(8,128)(2,1)}, u32[]{:S(2)}) copy-start(bf16[32,128,256]{2,1,0:T(8,128)(2,1)} %param.7) | copy-start | bytes 6291460
  2.9 7.7 %collective-permute-start = (bf16[1,32,8,256]{3,1,2,0:T(8,128)(2,1)S(1)}, bf16[1,32,8,256]{3,1,2,0:T(8,128)(2,1)S(1)}, u32[]{:S(2)}, u32[]{:S(2)}) collective-permute-start(bf16[1,32,8,256]{3,1,2,0:T(8,128)(2,1)S(1)} %get-tuple-element.15), channel_id=1, source_target_pairs={{0,4},{4,8},{8,12},{12,16},{16,20},{20,24},{24,28},{1,5},{5,9},{9,... | collective-permute-start | bytes 393224 | tf_op jit(solution)/shard_map/ppermute | solution.py:18
  5.3 5.3 %collective-permute-start.1 = (bf16[1,32,8,256]{3,1,2,0:T(8,128)(2,1)S(1)}, bf16[1,32,8,256]{3,1,2,0:T(8,128)(2,1)S(1)}, u32[]{:S(2)}, u32[]{:S(2)}) collective-permute-start(bf16[1,32,8,256]{3,1,2,0:T(8,128)(2,1)S(1)} %get-tuple-element.16), channel_id=1, source_target_pairs={{4,0},{8,4},{12,8},{16,12},{20,16},{24,20},{28,24},{5,1},{9,5},{13... | collective-permute-start | bytes 393224 | tf_op jit(solution)/shard_map/ppermute | solution.py:20
  15.8 15.3 %collective-permute-start.2 = (bf16[1,32,144,8]{2,3,1,0:T(8,128)(2,1)}, bf16[1,32,144,8]{2,3,1,0:T(8,128)(2,1)}, u32[]{:S(2)}, u32[]{:S(2)}) collective-permute-start(bf16[1,32,144,8]{2,3,1,0:T(8,128)(2,1)} %copy.40), channel_id=1, source_target_pairs={{0,1},{1,2},{2,3},{4,5},{5,6},{6,7},{8,9},{9,10},{10,11},{12,13},{... | collective-permute-start | bytes 221192 | tf_op jit(solution)/shard_map/ppermute | solution.py:18
  22.8 10.8 %collective-permute-start.3 = (bf16[1,32,144,8]{2,3,1,0:T(8,128)(2,1)}, bf16[1,32,144,8]{2,3,1,0:T(8,128)(2,1)}, u32[]{:S(2)}, u32[]{:S(2)}) collective-permute-start(bf16[1,32,144,8]{2,3,1,0:T(8,128)(2,1)} %copy.42), channel_id=1, source_target_pairs={{1,0},{2,1},{3,2},{5,4},{6,5},{7,6},{9,8},{10,9},{11,10},{13,12},{... | collective-permute-start | bytes 221192 | tf_op jit(solution)/shard_map/ppermute | solution.py:20
  37.1 7.1 %copy-start.8 = (bf16[3,3,32,32]{3,2,1,0:T(8,128)(2,1)S(1)}, bf16[3,3,32,32]{3,2,1,0:T(8,128)(2,1)}, u32[]{:S(2)}) copy-start(bf16[3,3,32,32]{3,2,1,0:T(8,128)(2,1)} %param.8) | copy-start | bytes 55300
  55.0 3.6 copy-start.5
  71.3 100.5 %copy-start.12 = (f32[32]{0:T(128)S(1)}, f32[32]{0:T(128)}, u32[]{:S(2)}) copy-start(f32[32]{0:T(128)} %param.10) | copy-start | bytes 388
  71.3 100.5 %copy-start.10 = (f32[32]{0:T(128)S(1)}, f32[32]{0:T(128)}, u32[]{:S(2)}) copy-start(f32[32]{0:T(128)} %param.11) | copy-start | bytes 388
  171.8 5.8 %copy-start = (f32[32,128,256]{2,0,1:T(8,128)S(1)}, f32[32,128,256]{2,0,1:T(8,128)}, u32[]{:S(2)}) copy-start(f32[32,128,256]{2,0,1:T(8,128)} %get-tuple-element.18) | copy-start | bytes 12582916
  175.0 6.1 %collective-permute-start.4 = (bf16[1,32,8,256]{3,1,2,0:T(8,128)(2,1)S(1)}, bf16[1,32,8,256]{3,1,2,0:T(8,128)(2,1)S(1)}, u32[]{:S(2)}, u32[]{:S(2)}) collective-permute-start(bf16[1,32,8,256]{3,1,2,0:T(8,128)(2,1)S(1)} %get-tuple-element.13), channel_id=1, source_target_pairs={{0,4},{4,8},{8,12},{12,16},{16,20},{20,24},{24,28},{1,5},{5,9},{9,... | collective-permute-start | bytes 393224 | tf_op jit(solution)/shard_map/ppermute | solution.py:18
  176.3 5.7 %collective-permute-start.5 = (bf16[1,32,8,256]{3,1,2,0:T(8,128)(2,1)S(1)}, bf16[1,32,8,256]{3,1,2,0:T(8,128)(2,1)S(1)}, u32[]{:S(2)}, u32[]{:S(2)}) collective-permute-start(bf16[1,32,8,256]{3,1,2,0:T(8,128)(2,1)S(1)} %get-tuple-element.14), channel_id=1, source_target_pairs={{4,0},{8,4},{12,8},{16,12},{20,16},{24,20},{28,24},{5,1},{9,5},{13... | collective-permute-start | bytes 393224 | tf_op jit(solution)/shard_map/ppermute | solution.py:20
  187.2 12.7 %collective-permute-start.6 = (bf16[1,32,144,8]{2,3,1,0:T(8,128)(2,1)}, bf16[1,32,144,8]{2,3,1,0:T(8,128)(2,1)}, u32[]{:S(2)}, u32[]{:S(2)}) collective-permute-start(bf16[1,32,144,8]{2,3,1,0:T(8,128)(2,1)} %copy.45), channel_id=1, source_target_pairs={{0,1},{1,2},{2,3},{4,5},{5,6},{6,7},{8,9},{9,10},{10,11},{12,13},{... | collective-permute-start | bytes 221192 | tf_op jit(solution)/shard_map/ppermute | solution.py:18
  192.0 10.5 %collective-permute-start.7 = (bf16[1,32,144,8]{2,3,1,0:T(8,128)(2,1)}, bf16[1,32,144,8]{2,3,1,0:T(8,128)(2,1)}, u32[]{:S(2)}, u32[]{:S(2)}) collective-permute-start(bf16[1,32,144,8]{2,3,1,0:T(8,128)(2,1)} %copy.47), channel_id=1, source_target_pairs={{1,0},{2,1},{3,2},{5,4},{6,5},{7,6},{9,8},{10,9},{11,10},{13,12},{... | collective-permute-start | bytes 221192 | tf_op jit(solution)/shard_map/ppermute | solution.py:20
  205.9 7.1 %copy-start.9 = (bf16[3,3,32,32]{3,2,1,0:T(8,128)(2,1)S(1)}, bf16[3,3,32,32]{3,2,1,0:T(8,128)(2,1)}, u32[]{:S(2)}) copy-start(bf16[3,3,32,32]{3,2,1,0:T(8,128)(2,1)} %param.9) | copy-start | bytes 55300
  220.9 5.6 %copy-start.7 = (f32[128,256,32]{1,2,0:T(8,128)S(1)}, f32[128,256,32]{1,2,0:T(8,128)}, u32[]{:S(2)}) copy-start(f32[128,256,32]{1,2,0:T(8,128)} %fusion.5) | copy-start | bytes 12582916
  223.7 3.2 copy-start.6
  238.4 88.5 %copy-start.13 = (f32[32]{0:T(128)S(1)}, f32[32]{0:T(128)}, u32[]{:S(2)}) copy-start(f32[32]{0:T(128)} %param.12) | copy-start | bytes 388
  238.4 88.5 %copy-start.2 = (bf16[32,128,256]{2,1,0:T(8,128)(2,1)S(1)}, bf16[32,128,256]{2,1,0:T(8,128)(2,1)}, u32[]{:S(2)}) copy-start(bf16[32,128,256]{2,1,0:T(8,128)(2,1)} %param.7) | copy-start | bytes 6291460
  238.4 88.5 %copy-start.11 = (f32[32]{0:T(128)S(1)}, f32[32]{0:T(128)}, u32[]{:S(2)}) copy-start(f32[32]{0:T(128)} %param.13) | copy-start | bytes 388
  330.9 52.4 %copy-start.3 = (bf16[32,128,256]{2,0,1:T(8,128)(2,1)}, bf16[32,128,256]{2,0,1:T(8,128)(2,1)S(1)}, u32[]{:S(2)}) copy-start(bf16[32,128,256]{2,0,1:T(8,128)(2,1)S(1)} %fusion.2) | copy-start | bytes 6291460
  506.4 5.6 %copy-start.4 = (bf16[32,128,256]{2,0,1:T(8,128)(2,1)S(1)}, bf16[32,128,256]{2,0,1:T(8,128)(2,1)}, u32[]{:S(2)}) copy-start(bf16[32,128,256]{2,0,1:T(8,128)(2,1)} %copy-done.3) | copy-start | bytes 6291460
where the time goes:
time: 525 us; the launch traced here: 518 us
  blocking collectives  315 us (60%)
  local copies, waits for them, and re-layouts  81.8 us (16%)
  matrix products  72 us (14%)
  other arithmetic  31.2 us (6%)
  starting transfers between devices  16.7 us (3%)
    psum x2, blocking collectives, channel_affine(): lax.psum(jnp.sum(deviation * deviation, axis=(1, 2)), ('row', 'col'))  95.6 us
    psum x2, blocking collectives, channel_affine(): sums = lax.psum(jnp.sum(inner, axis=(1, 2)), ('row', 'col'))  87.6 us
    dot_general x18, matrix products, apply_taps(): jnp.einsum('poc,pchw->pohw', kernels[:, filter_row, filter_column], piece...  72 us
    all_to_all x1, blocking collectives, mirror(): lax.all_to_all(block, 'col', split_axis=1, concat_axis=2, tiled=True)  50.7 us
    all_to_all x1, blocking collectives, mirror(): lax.all_to_all(lax.all_to_all(banded, 'row', split_axis=2, concat_axis=1,...  50.5 us
    all_to_all x1, blocking collectives, mirror(): lax.all_to_all(banded, 'row', split_axis=2, concat_axis=1, tiled=True)  30.1 us
    unnamed x31, local copies, waits for them, and re-layouts  23.1 us
    concatenate x4, other arithmetic, with_halo(): jnp.concatenate([lax.ppermute(tail, axis, [(i, (i + 1) % count) for i in...  14.8 us
  transfers between devices with their start and end apart: 8, of which 1 were waited for; matrix products, arithmetic and copies ran while one was open for 6% of the time, Pallas kernels for 0%

commit v1 on v0

--- a/solution.py
+++ b/solution.py
@@ -50,7 +50,8 @@
 
 
 def channel_affine(inner, gain, total_cells):
-    sums = lax.psum(jnp.sum(inner, axis=(1, 2)), ("row", "col"))
+    half = lax.psum(jnp.sum(inner, axis=(1, 2)), "col")
+    sums = lax.psum(half, "row")
     centre = sums / total_cells
     deviation = inner - centre[:, None, None]
     spread = lax.psum(jnp.sum(deviation * deviation, axis=(1, 2)), ("row", "col")) / total_cells

time: 525 us -> 474 us (0.903)
  blocking collectives: 315 us -> 261 us
    psum x2 -> x4, blocking collectives: 87.6 us -> 52.5 us  [the longest x2 28.3 us: channel_affine(): sums = lax.psum(half, 'row')]
    psum x2, blocking collectives: 95.6 us -> 75.8 us  [channel_affine(): lax.psum(jnp.sum(deviation * deviation, axis=(1, 2)), ('row', 'col'))]
where the time goes in v1:
time: 474 us; the launch traced here: 467 us
  blocking collectives  261 us (55%)
  local copies, waits for them, and re-layouts  81.7 us (17%)
  matrix products  72.1 us (15%)
  other arithmetic  31.2 us (7%)
  starting transfers between devices  19.7 us (4%)
    psum x2, blocking collectives, channel_affine(): lax.psum(jnp.sum(deviation * deviation, axis=(1, 2)), ('row', 'col'))  75.8 us
    dot_general x18, matrix products, apply_taps(): jnp.einsum('poc,pchw->pohw', kernels[:, filter_row, filter_column], piece...  72.1 us
    all_to_all x1, blocking collectives, mirror(): lax.all_to_all(block, 'col', split_axis=1, concat_axis=2, tiled=True)  51.4 us
    all_to_all x1, blocking collectives, mirror(): lax.all_to_all(lax.all_to_all(banded, 'row', split_axis=2, concat_axis=1,...  50.5 us
    all_to_all x1, blocking collectives, mirror(): lax.all_to_all(banded, 'row', split_axis=2, concat_axis=1, tiled=True)  30.5 us
    psum x2, blocking collectives, channel_affine(): sums = lax.psum(half, 'row')  28.3 us
    psum x2, blocking collectives, channel_affine(): half = lax.psum(jnp.sum(inner, axis=(1, 2)), 'col')  24.2 us
    unnamed x31, local copies, waits for them, and re-layouts  23 us
  transfers between devices with their start and end apart: 8, of which 1 were waited for; matrix products, arithmetic and copies ran while one was open for 6% of the time, Pallas kernels for 0%

profile of v1, /device:TPU:0, one launch (start us, length us, event | category | flops | bytes accessed | tf_op | source)
XLA Modules:
  0.0 467.1 jit_solution(9106376276695265468)
XLA Ops:
  0.0 2.9 copy.68
  6.6 4.0 fusion.30
  12.6 3.2 copy.40
  15.8 4.9 %collective-permute-start.2 = (bf16[1,32,144,8]{2,3,1,0:T(8,128)(2,1)}, bf16[1,32,144,8]{2,3,1,0:T(8,128)(2,1)}, u32[]{:S(2)}, u32[]{:S(2)}) collective-permute-start(bf16[1,32,144,8]{2,3,1,0:T(8,128)(2,1)} %copy.40), channel_id=1, source_target_pairs={{0,1},{1,2},{2,3},{4,5},{5,6},{6,7},{8,9},{9,10},{10,11},{12,13},{... | collective-permute-start | bytes 221192 | tf_op jit(solution)/shard_map/ppermute | solution.py:18
  24.6 3.4 fusion.18
  28.0 3.3 fusion.26
  31.3 2.6 copy.41
  33.9 3.4 copy.43
  37.3 7.1 %pad_maximum_fusion = (bf16[1,32,144,264]{3,1,2,0:T(8,128)(2,1)S(1)}, bf16[1,32,144,264]{3,1,2,0:T(8,128)(2,1)S(1)}) fusion(bf16[1,32,144,8]{3,1,2,0:T(8,128)(2,1)} %copy.43, bf16[1,32,8,256]{3,1,2,0:T(8,128)(2,1)S(1)} %collective-permute-done.1, bf16[1,32,128,256]{3,1,2,0:T(8,128)(2,1)S(1)} %bitcast.206, ...), kind=kLoop, calls=%fused_computation.16 | loop fusion | flops 19464192 | bytes 7372800 | tf_op jit(solution)/shard_map/concatenate | solution.py:16
  44.5 2.7 fusion.21
  47.1 2.6 fusion.23
  49.7 2.8 fusion.22
  52.5 2.8 fusion.24
  55.3 2.8 fusion.29
  58.9 12.7 %fusion.41 = (f32[32]{0:T(128)S(1)}, f32[32,128,256]{2,0,1:T(8,128)}) fusion(bf16[1,32,144,264]{3,1,2,0:T(8,128)(2,1)S(1)} %get-tuple-element.9, bf16[1,3,3,32,32]{4,3,2,1,0:T(8,128)(2,1)} %bitcast.217, f32[128,256,32]{1,2,0:T(8,128)S(1)} %copy-done.5, f32[128,256,32]{1,2,0:T(8,128)} %fusion.21, f32[128,256,32]{1,2,0:T(8,128)} %fusion.22, ...), kind=kOutput, calls=%fused_computation.95 | convolution fusion | flops 76546016 | bytes 39854208 | tf_op jit(solution)/shard_map/poc,pchw->pohw/dot_general | solution.py:39
  71.6 13.0 %psum.42 = f32[32]{0:T(128)S(1)} all-reduce(f32[32]{0:T(128)S(1)} %get-tuple-element.17), channel_id=1, replica_groups=mesh['row'=8,'col'=4] {'col'}, use_global_device_ids=true, to_apply=%region_1.0 | all-reduce | flops 32 | bytes 256 | tf_op jit(solution)/shard_map/psum | solution.py:53
  84.6 13.7 %psum.43 = f32[32]{0:T(128)S(1)} all-reduce(f32[32]{0:T(128)S(1)} %psum.42), channel_id=1, replica_groups=mesh['row'=8,'col'=4] {'row'}, use_global_device_ids=true, to_apply=%region_2.0 | all-reduce | flops 32 | bytes 256 | tf_op jit(solution)/shard_map/psum | solution.py:54
  98.3 2.8 multiply_reduce_fusion.1
  101.2 38.1 %psum.44 = f32[32]{0:T(128)S(1)} all-reduce(f32[32]{0:T(128)S(1)} %multiply_reduce_fusion.1), channel_id=1, replica_groups=mesh['row'=8,'col'=4] {'row','col'}, use_global_device_ids=true, to_apply=%region_4.0 | all-reduce | flops 32 | bytes 256 | tf_op jit(solution)/shard_map/psum | solution.py:57
  139.3 3.1 fusion.44
  145.0 3.5 fusion.32
  151.4 3.2 copy.45
  154.6 5.4 %collective-permute-start.6 = (bf16[1,32,144,8]{2,3,1,0:T(8,128)(2,1)}, bf16[1,32,144,8]{2,3,1,0:T(8,128)(2,1)}, u32[]{:S(2)}, u32[]{:S(2)}) collective-permute-start(bf16[1,32,144,8]{2,3,1,0:T(8,128)(2,1)} %copy.45), channel_id=1, source_target_pairs={{0,1},{1,2},{2,3},{4,5},{5,6},{6,7},{8,9},{9,10},{10,11},{12,13},{... | collective-permute-start | bytes 221192 | tf_op jit(solution)/shard_map/ppermute | solution.py:18
  163.4 3.3 fusion.13
  166.7 3.3 fusion.5
  172.7 3.4 copy.48
  176.1 7.1 %pad_maximum_fusion.1 = (bf16[1,32,144,264]{3,1,2,0:T(8,128)(2,1)S(1)}, bf16[1,32,144,264]{3,1,2,0:T(8,128)(2,1)S(1)}) fusion(bf16[1,32,144,8]{3,1,2,0:T(8,128)(2,1)} %copy.48, bf16[1,32,8,256]{3,1,2,0:T(8,128)(2,1)S(1)} %collective-permute-done.5, bf16[1,32,128,256]{3,1,2,0:T(8,128)(2,1)S(1)} %fusion.44, ...), kind=kLoop, calls=%fused_computation.18 | loop fusion | flops 19464192 | bytes 7372800 | tf_op jit(solution)/shard_map/concatenate | solution.py:16
  183.2 2.7 fusion.10
  185.9 2.6 fusion.16
  188.5 2.6 fusion.8
  191.1 2.8 fusion.11
  193.9 2.8 fusion.9
  197.1 11.5 %fusion.42 = (f32[32]{0:T(128)S(1)}, f32[128,256,32]{1,2,0:T(8,128)}) fusion(bf16[1,32,144,264]{3,1,2,0:T(8,128)(2,1)S(1)} %get-tuple-element.5, bf16[1,3,3,32,32]{4,3,2,1,0:T(8,128)(2,1)} %bitcast.226, f32[128,256,32]{1,2,0:T(8,128)S(1)} %copy-done.7, f32[128,256,32]{1,2,0:T(8,128)} %fusion.8, f32[128,256,32]{1,2,0:T(8,128)} %fusion.9, ...), kind=kOutput, calls=%fused_computation.96 | convolution fusion | flops 76546016 | bytes 39854208 | tf_op jit(solution)/shard_map/poc,pchw->pohw/dot_general | solution.py:39
  208.6 11.1 %psum.45 = f32[32]{0:T(128)S(1)} all-reduce(f32[32]{0:T(128)S(1)} %get-tuple-element.19), channel_id=1, replica_groups=mesh['row'=8,'col'=4] {'col'}, use_global_device_ids=true, to_apply=%region_6.0 | all-reduce | flops 32 | bytes 256 | tf_op jit(solution)/shard_map/psum | solution.py:53
  219.8 14.5 %psum.46 = f32[32]{0:T(128)S(1)} all-reduce(f32[32]{0:T(128)S(1)} %psum.45), channel_id=1, replica_groups=mesh['row'=8,'col'=4] {'row'}, use_global_device_ids=true, to_apply=%region_7.0 | all-reduce | flops 32 | bytes 256 | tf_op jit(solution)/shard_map/psum | solution.py:54
  234.3 2.8 multiply_reduce_fusion
  237.2 37.7 %psum.47 = f32[32]{0:T(128)S(1)} all-reduce(f32[32]{0:T(128)S(1)} %multiply_reduce_fusion), channel_id=1, replica_groups=mesh['row'=8,'col'=4] {'row','col'}, use_global_device_ids=true, to_apply=%region_9.0 | all-reduce | flops 32 | bytes 256 | tf_op jit(solution)/shard_map/psum | solution.py:57
  274.9 4.0 fusion.2
  278.9 51.4 %all_to_all.41 = bf16[32,128,256]{2,0,1:T(8,128)(2,1)S(1)} all-to-all(bf16[32,128,256]{2,0,1:T(8,128)(2,1)S(1)} %fusion.2), channel_id=1, replica_groups=mesh['row'=8,'col'=4] {'col'}, dimensions={1} | all-to-all | bytes 4194304 | tf_op jit(solution)/shard_map/all_to_all | solution.py:90
  331.9 7.1 %copy.58 = bf16[32,32,4,256]{1,0,3,2:T(8,128)(2,1)} copy(bf16[32,32,4,256]{3,2,1,0:T(4,128)(2,1)S(1)} %bitcast.210) | data formatting | bytes 4194304 | tf_op jit(solution)/shard_map/all_to_all | solution.py:90
  339.0 10.1 %reshape.252 = bf16[8,2,65536]{2,1,0:T(2,128)(2,1)S(1)} reshape(bf16[1024,32,32]{2,1,0:T(8,128)(2,1)} %bitcast.207) | data formatting | bytes 4194304
  349.2 30.5 %all_to_all.42 = bf16[8,2,65536]{2,1,0:T(2,128)(2,1)} all-to-all(bf16[8,2,65536]{2,1,0:T(2,128)(2,1)S(1)} %reshape.252), channel_id=1, replica_groups=mesh['row'=8,'col'=4] {'row'}, dimensions={0} | all-to-all | bytes 4194304 | tf_op jit(solution)/shard_map/all_to_all | solution.py:92
  379.7 8.7 %reshape.253 = bf16[1024,32,32]{2,1,0:T(8,128)(2,1)} reshape(bf16[8,2,65536]{2,1,0:T(2,128)(2,1)} %all_to_all.42) | data formatting | bytes 4194304
  388.4 12.6 %copy.61 = bf16[32,8,32,128]{3,0,2,1:T(8,128)(2,1)S(1)} copy(bf16[32,8,32,128]{2,0,3,1:T(8,128)(2,1)} %bitcast.208) | data formatting | bytes 4194304 | tf_op jit(solution)/shard_map/all_to_all | solution.py:92
  400.9 50.5 %all_to_all.43 = bf16[32,256,128]{2,0,1:T(8,128)(2,1)S(1)} all-to-all(bf16[32,256,128]{2,0,1:T(8,128)(2,1)S(1)} %bitcast.211), channel_id=1, replica_groups=mesh['row'=8,'col'=4] {'col'}, dimensions={1} | all-to-all | bytes 4194304 | tf_op jit(solution)/shard_map/all_to_all | solution.py:91
  452.9 2.6 copy.55
  455.5 5.6 %copy.56 = f32[32,256,128]{1,0,2:T(8,128)} copy(f32[32,256,128]{2,1,0:T(8,128)} %bitcast.209) | data formatting | bytes 8388608 | tf_op jit(solution)/shard_map/convert_element_type | solution.py:115
  461.1 3.0 fusion.1
  (59 shorter events, 27.7 us)
Async XLA Ops:
  0.0 6.6 %copy-start.1 = (bf16[32,128,256]{2,1,0:T(8,128)(2,1)S(1)}, bf16[32,128,256]{2,1,0:T(8,128)(2,1)}, u32[]{:S(2)}) copy-start(bf16[32,128,256]{2,1,0:T(8,128)(2,1)} %param.7) | copy-start | bytes 6291460
  2.9 7.7 %collective-permute-start = (bf16[1,32,8,256]{3,1,2,0:T(8,128)(2,1)S(1)}, bf16[1,32,8,256]{3,1,2,0:T(8,128)(2,1)S(1)}, u32[]{:S(2)}, u32[]{:S(2)}) collective-permute-start(bf16[1,32,8,256]{3,1,2,0:T(8,128)(2,1)S(1)} %get-tuple-element.15), channel_id=1, source_target_pairs={{0,4},{4,8},{8,12},{12,16},{16,20},{20,24},{24,28},{1,5},{5,9},{9,... | collective-permute-start | bytes 393224 | tf_op jit(solution)/shard_map/ppermute | solution.py:18
  5.3 5.3 %collective-permute-start.1 = (bf16[1,32,8,256]{3,1,2,0:T(8,128)(2,1)S(1)}, bf16[1,32,8,256]{3,1,2,0:T(8,128)(2,1)S(1)}, u32[]{:S(2)}, u32[]{:S(2)}) collective-permute-start(bf16[1,32,8,256]{3,1,2,0:T(8,128)(2,1)S(1)} %get-tuple-element.16), channel_id=1, source_target_pairs={{4,0},{8,4},{12,8},{16,12},{20,16},{24,20},{28,24},{5,1},{9,5},{13... | collective-permute-start | bytes 393224 | tf_op jit(solution)/shard_map/ppermute | solution.py:20
  15.8 15.5 %collective-permute-start.2 = (bf16[1,32,144,8]{2,3,1,0:T(8,128)(2,1)}, bf16[1,32,144,8]{2,3,1,0:T(8,128)(2,1)}, u32[]{:S(2)}, u32[]{:S(2)}) collective-permute-start(bf16[1,32,144,8]{2,3,1,0:T(8,128)(2,1)} %copy.40), channel_id=1, source_target_pairs={{0,1},{1,2},{2,3},{4,5},{5,6},{6,7},{8,9},{9,10},{10,11},{12,13},{... | collective-permute-start | bytes 221192 | tf_op jit(solution)/shard_map/ppermute | solution.py:18
  22.8 11.1 %collective-permute-start.3 = (bf16[1,32,144,8]{2,3,1,0:T(8,128)(2,1)}, bf16[1,32,144,8]{2,3,1,0:T(8,128)(2,1)}, u32[]{:S(2)}, u32[]{:S(2)}) collective-permute-start(bf16[1,32,144,8]{2,3,1,0:T(8,128)(2,1)} %copy.42), channel_id=1, source_target_pairs={{1,0},{2,1},{3,2},{5,4},{6,5},{7,6},{9,8},{10,9},{11,10},{13,12},{... | collective-permute-start | bytes 221192 | tf_op jit(solution)/shard_map/ppermute | solution.py:20
  37.3 7.1 %copy-start.8 = (bf16[3,3,32,32]{3,2,1,0:T(8,128)(2,1)S(1)}, bf16[3,3,32,32]{3,2,1,0:T(8,128)(2,1)}, u32[]{:S(2)}) copy-start(bf16[3,3,32,32]{3,2,1,0:T(8,128)(2,1)} %param.8) | copy-start | bytes 55300
  55.3 3.6 copy-start.5
  71.5 67.7 %copy-start.12 = (f32[32]{0:T(128)S(1)}, f32[32]{0:T(128)}, u32[]{:S(2)}) copy-start(f32[32]{0:T(128)} %param.10) | copy-start | bytes 388
  71.5 67.7 %copy-start.10 = (f32[32]{0:T(128)S(1)}, f32[32]{0:T(128)}, u32[]{:S(2)}) copy-start(f32[32]{0:T(128)} %param.11) | copy-start | bytes 388
  139.2 5.8 %copy-start = (f32[32,128,256]{2,0,1:T(8,128)S(1)}, f32[32,128,256]{2,0,1:T(8,128)}, u32[]{:S(2)}) copy-start(f32[32,128,256]{2,0,1:T(8,128)} %get-tuple-element.18) | copy-start | bytes 12582916
  142.4 6.1 %collective-permute-start.4 = (bf16[1,32,8,256]{3,1,2,0:T(8,128)(2,1)S(1)}, bf16[1,32,8,256]{3,1,2,0:T(8,128)(2,1)S(1)}, u32[]{:S(2)}, u32[]{:S(2)}) collective-permute-start(bf16[1,32,8,256]{3,1,2,0:T(8,128)(2,1)S(1)} %get-tuple-element.13), channel_id=1, source_target_pairs={{0,4},{4,8},{8,12},{12,16},{16,20},{20,24},{24,28},{1,5},{5,9},{9,... | collective-permute-start | bytes 393224 | tf_op jit(solution)/shard_map/ppermute | solution.py:18
  143.7 5.7 %collective-permute-start.5 = (bf16[1,32,8,256]{3,1,2,0:T(8,128)(2,1)S(1)}, bf16[1,32,8,256]{3,1,2,0:T(8,128)(2,1)S(1)}, u32[]{:S(2)}, u32[]{:S(2)}) collective-permute-start(bf16[1,32,8,256]{3,1,2,0:T(8,128)(2,1)S(1)} %get-tuple-element.14), channel_id=1, source_target_pairs={{4,0},{8,4},{12,8},{16,12},{20,16},{24,20},{28,24},{5,1},{9,5},{13... | collective-permute-start | bytes 393224 | tf_op jit(solution)/shard_map/ppermute | solution.py:20
  154.6 15.4 %collective-permute-start.6 = (bf16[1,32,144,8]{2,3,1,0:T(8,128)(2,1)}, bf16[1,32,144,8]{2,3,1,0:T(8,128)(2,1)}, u32[]{:S(2)}, u32[]{:S(2)}) collective-permute-start(bf16[1,32,144,8]{2,3,1,0:T(8,128)(2,1)} %copy.45), channel_id=1, source_target_pairs={{0,1},{1,2},{2,3},{4,5},{5,6},{6,7},{8,9},{9,10},{10,11},{12,13},{... | collective-permute-start | bytes 221192 | tf_op jit(solution)/shard_map/ppermute | solution.py:18
  162.1 10.5 %collective-permute-start.7 = (bf16[1,32,144,8]{2,3,1,0:T(8,128)(2,1)}, bf16[1,32,144,8]{2,3,1,0:T(8,128)(2,1)}, u32[]{:S(2)}, u32[]{:S(2)}) collective-permute-start(bf16[1,32,144,8]{2,3,1,0:T(8,128)(2,1)} %copy.47), channel_id=1, source_target_pairs={{1,0},{2,1},{3,2},{5,4},{6,5},{7,6},{9,8},{10,9},{11,10},{13,12},{... | collective-permute-start | bytes 221192 | tf_op jit(solution)/shard_map/ppermute | solution.py:20
  176.1 7.1 %copy-start.9 = (bf16[3,3,32,32]{3,2,1,0:T(8,128)(2,1)S(1)}, bf16[3,3,32,32]{3,2,1,0:T(8,128)(2,1)}, u32[]{:S(2)}) copy-start(bf16[3,3,32,32]{3,2,1,0:T(8,128)(2,1)} %param.9) | copy-start | bytes 55300
  191.1 5.6 %copy-start.7 = (f32[128,256,32]{1,2,0:T(8,128)S(1)}, f32[128,256,32]{1,2,0:T(8,128)}, u32[]{:S(2)}) copy-start(f32[128,256,32]{1,2,0:T(8,128)} %fusion.5) | copy-start | bytes 12582916
  193.9 3.2 copy-start.6
  208.6 66.3 %copy-start.13 = (f32[32]{0:T(128)S(1)}, f32[32]{0:T(128)}, u32[]{:S(2)}) copy-start(f32[32]{0:T(128)} %param.12) | copy-start | bytes 388
  208.6 66.3 %copy-start.2 = (bf16[32,128,256]{2,1,0:T(8,128)(2,1)S(1)}, bf16[32,128,256]{2,1,0:T(8,128)(2,1)}, u32[]{:S(2)}) copy-start(bf16[32,128,256]{2,1,0:T(8,128)(2,1)} %param.7) | copy-start | bytes 6291460
  208.6 66.3 %copy-start.11 = (f32[32]{0:T(128)S(1)}, f32[32]{0:T(128)}, u32[]{:S(2)}) copy-start(f32[32]{0:T(128)} %param.13) | copy-start | bytes 388
  278.9 53.0 %copy-start.3 = (bf16[32,128,256]{2,0,1:T(8,128)(2,1)}, bf16[32,128,256]{2,0,1:T(8,128)(2,1)S(1)}, u32[]{:S(2)}) copy-start(bf16[32,128,256]{2,0,1:T(8,128)(2,1)S(1)} %fusion.2) | copy-start | bytes 6291460
  455.5 5.7 %copy-start.4 = (bf16[32,128,256]{2,0,1:T(8,128)(2,1)S(1)}, bf16[32,128,256]{2,0,1:T(8,128)(2,1)}, u32[]{:S(2)}) copy-start(bf16[32,128,256]{2,0,1:T(8,128)(2,1)} %copy-done.3) | copy-start | bytes 6291460
